TPU v7x, 512 devices: a whole 4x4x16 slice. The times are simulated.
512 devices in a mesh: rep: 16 (over x, z_hi, core), fsdp: 32 (over y, z_lo).
Axes of the slice: x: 4, y: 4, z: 16 (z_hi: 2, z_lo: 8; z = z_hi * 8 + z_lo), core: 2. Of those that a mesh axis runs over, the one named last changes fastest.
Arguments:
- inner: bfloat16 [16, 1, 8192, 2048], P('rep', None, 'fsdp'), may hold values from -6 to 6
- anchor: bfloat16 [1, 8192, 2048], P(None, 'fsdp'), may hold values from -6 to 6
- exponent: int32 [16, 1, 8192, 64], P('rep', None, 'fsdp'), may hold values from -1 to 1
- momentum: float32 [1, 8192, 2048], P(None, 'fsdp', 'rep'), may hold values from -4 to 4
Outputs:
- mixed: bfloat16 [16, 1, 8192, 2048], P('rep', None, 'fsdp')
- new_anchor: bfloat16 [1, 8192, 2048], P(None, 'fsdp')
- momentum_next: float32 [1, 8192, 2048], P(None, 'fsdp', 'rep')
All inputs are finite; a program needn't handle non-finite values.
Results may differ from a plain program's by a relative error of at most 0.0035.
Values may be sent and summed in bfloat16 or wider, within the bound.
A program may use at most 64 MiB of HBM per device.

v0:
```python
import jax
import jax.numpy as jnp
from jax import lax
from jax.sharding import PartitionSpec as P

levels_table = (
    (0.25, 0.5),
    (0.75, 0.5),
    (1.25, 0.5),
    (1.75, 0.5),
    (2.5, 1.0),
    (3.5, 1.0),
    (5.0, 2.0),
)


def block_scale(exponent):
    scale = jnp.zeros(exponent.shape, jnp.float32)
    for power in (-1, 0, 1):
        scale = scale + jnp.where(exponent == power, jnp.float32(2.0**power), jnp.float32(0.0))
    return scale


def encode(delta, exponent):
    shape = delta.shape
    blocks = delta.reshape(shape[:-1] + (shape[-1] // 32, 32))
    scale = block_scale(exponent)[..., None]
    magnitude = jnp.abs(blocks) / scale
    level = jnp.zeros(blocks.shape, jnp.float32)
    for bound, height in levels_table:
        level = level + jnp.where(magnitude >= bound, jnp.float32(height), jnp.float32(0.0))
    signed = jnp.where(blocks < 0, -level, level) * scale
    return signed.reshape(shape).astype(jnp.bfloat16)


def on_device(inner, anchor, exponent, momentum):
    replicas = lax.axis_size("rep")
    layers, rows, width = anchor.shape
    share = width // replicas
    anchor_wide = anchor.astype(jnp.float32)
    delta = anchor_wide - inner[0].astype(jnp.float32)
    coded = encode(delta, exponent[0])
    total = lax.psum_scatter(
        coded.astype(jnp.float32).astype(jnp.bfloat16), "rep", scatter_dimension=2, tiled=True
    ).astype(jnp.float32)
    outer_grad = total / replicas
    start = lax.axis_index("rep") * share
    own = lax.dynamic_slice_in_dim(anchor_wide, start, share, 2)
    momentum_next = 0.9 * momentum + outer_grad
    shard_new = (own - 0.7 * (outer_grad + 0.9 * momentum_next)).astype(jnp.bfloat16)
    new_anchor = lax.all_gather(shard_new, "rep", axis=2, tiled=True)
    mixed = (0.5 * inner.astype(jnp.float32) + 0.5 * new_anchor.astype(jnp.float32)[None]).astype(
        jnp.bfloat16
    )
    return (mixed, new_anchor, momentum_next)


def solution(mesh):
    return jax.shard_map(
        on_device,
        mesh=mesh,
        in_specs=(
            P("rep", None, "fsdp", None),
            P(None, "fsdp", None),
            P("rep", None, "fsdp", None),
            P(None, "fsdp", "rep"),
        ),
        out_specs=(P("rep", None, "fsdp", None), P(None, "fsdp", None), P(None, "fsdp", "rep")),
        check_vma=False,
    )
```

profile of v0, /device:TPU:1, one launch (start us, length us, event | category | flops | bytes accessed | tf_op | source)
XLA Modules:
  0.0 210.7 jit_solution(16514815856788452866)
XLA Ops:
  7.2 0.0 copy-start.1
  7.2 0.0 copy-start.3
  7.2 0.0 reduce-scatter.2.cloned.1.call-start
  7.2 1.6 copy.8
  8.8 0.0 copy-done.1
  8.8 0.5 copy.9
  9.3 0.0 copy-done.3
  9.4 3.0 %fusion.3 = bf16[1,256,2048]{1,2,0:T(8,128)(2,1)} fusion(bf16[1,1,256,2048]{2,3,1,0:T(8,128)(2,1)S(1)} %copy.8, f32[256,64]{0,1:T(8,128)S(1)} %add_bitcast_fusion, bf16[1,256,2048]{1,2,0:T(8,128)(2,1)S(1)} %copy.9), kind=kLoop, calls=%fused_computation.8 | loop fusion | flops 15728640 | bytes 3211264 | tf_op jit(solution)/shard_map/convert_element_type | solution.py:33
  12.4 0.0 copy-start.2
  12.4 0.0 reduce-scatter.2.cloned.1.call-update
  12.4 0.0 all-gather.2.cloned.1.call-start
  12.4 1.5 convert_element_type.38
  14.0 0.0 copy-done.2
  14.0 0.1 copy.10
  14.1 110.6 %reduce-scatter.2.cloned.1.call-done = bf16[1,256,128]{1,2,0:T(8,128)(2,1)} async-done(((bf16[1,256,2048]{1,2,0:T(8,128)(2,1)}), bf16[1,256,128]{1,2,0:T(8,128)(2,1)}) %reduce-scatter.2.cloned.1.call-update) | async-done | bytes 65552 | tf_op jit(solution)/shard_map/reduce_scatter | solution.py:43
  124.6 1.6 multiply_add_fusion
  126.3 0.0 all-gather.2.cloned.1.call-update
  126.3 0.8 copy.13
  127.0 72.4 %all-gather.2.cloned.1.call-done = bf16[1,256,2048]{1,2,0:T(8,128)(2,1)} async-done(((bf16[1,256,128]{1,2,0:T(8,128)(2,1)}), bf16[1,256,2048]{1,2,0:T(8,128)(2,1)}) %all-gather.2.cloned.1.call-update) | async-done | bytes 1048592 | tf_op jit(solution)/shard_map/all_gather | solution.py:51
  199.4 0.0 copy-start
  199.4 1.6 fusion.1
  201.1 1.4 copy.11
  202.5 0.0 copy-done
  202.5 1.4 copy.12
  (1 shorter events, 0.0 us)
Async XLA Ops:
  7.2 1.6 copy-start.1
  7.2 2.2 %copy-start.3 = (s32[1,1,256,64]{2,3,1,0:T(8,128)S(1)}, s32[1,1,256,64]{2,3,1,0:T(8,128)}, u32[]{:S(2)}) copy-start(s32[1,1,256,64]{2,3,1,0:T(8,128)} %param.6) | copy-start | bytes 196612
  7.2 117.5 %reduce-scatter.2.cloned.1.call-start = ((), (), s32[]{:S(2)}) async-start(), calls=%async_computation.1 | async-start | bytes 1114112 | tf_op jit(solution)/shard_map/reduce_scatter | solution.py:43
  12.4 1.6 copy-start.2
  12.4 187.0 %all-gather.2.cloned.1.call-start = ((), (), s32[]{:S(2)}) async-start(), calls=%async_computation.2 | async-start | bytes 1114112 | tf_op jit(solution)/shard_map/all_gather | solution.py:51
  199.4 3.1 %copy-start = (bf16[1,256,2048]{1,2,0:T(8,128)(2,1)S(1)}, bf16[1,256,2048]{1,2,0:T(8,128)(2,1)}, u32[]{:S(2)}) copy-start(bf16[1,256,2048]{1,2,0:T(8,128)(2,1)} %all-gather.2.cloned.1.call-done) | copy-start | bytes 3145732
Sparse Core Ops, SparseCore 0:
  13.3 111.3 reduce-scatter.1
  129.0 70.3 all-gather.1
where the time goes:
time: 211 us
  waiting for transfers between devices  183 us (87%)
  between operations  14.1 us (7%)
  other arithmetic  7.75 us (4%)
  local copies, waits for them, and re-layouts  5.79 us (3%)
    reduce_scatter x1, waiting for transfers between devices, on_device(): lax.psum_scatter(coded.astype(jnp.float32).astype(jnp.bfloat16), 'rep', s...  111 us
    all_gather x1, waiting for transfers between devices, on_device(): new_anchor = lax.all_gather(shard_new, 'rep', axis=2, tiled=True)  72.4 us
    unnamed x14, local copies, waits for them, and re-layouts  5.79 us
  transfers between devices with their start and end apart: 2, of which 2 were waited for; matrix products, arithmetic and copies ran while one was open for 1% of the time, Pallas kernels for 0%

commit v1 on v0

v1 whole, which is shorter than its diff:
```python
import functools

import jax
import jax.numpy as jnp
from jax import lax
from jax.experimental import pallas as pl
from jax.experimental.pallas import tpu as pltpu
from jax.sharding import PartitionSpec as P

MESH = pl.DeviceIdType.MESH
BLOCK = 32
LANE = 128
TILE = 16
GROUP = 8
REPS = 16
MINE, OTHER = 0.5, 0.7 * 1.9 / REPS
BOUNDS = ((0.25, 0.5), (0.75, 1.0), (1.25, 1.5), (1.75, 2.0), (2.5, 3.0), (3.5, 4.0), (5.0, 6.0))
CHUNKS = (4, 4, 4, 4)
PEERS = tuple((dx, dc) for dx in range(4) for dc in range(2) if (dx, dc) != (0, 0))


def column_of(group, half):
    return ((group // 2) * 4 + half * 2 + group % 2) * LANE


def spans():
    first = 0
    for k, tiles in enumerate(CHUNKS):
        yield k, first, tiles
        first += tiles


def exchange(
    inner,
    anchor,
    exponent,
    momentum,
    gathered,
    momentum_next,
    inner_v,
    anchor_v,
    exponent_v,
    spread,
    scale_v,
    inverse_v,
    coded,
    arrived,
    own_sum,
    z_out,
    z_in,
    load_sem,
    small_sem,
    rs_send,
    rs_recv,
    z_send,
    z_recv,
    ag_send,
    ag_recv,
    momentum_v,
):
    rep, fsdp = lax.axis_index("rep"), lax.axis_index("fsdp")
    x, half, core = rep // 4, (rep // 2) % 2, rep % 2
    group = x * 2 + core
    own_column = pl.multiple_of(rep * LANE, LANE)
    other_column = pl.multiple_of((x * 4 + (1 - half) * 2 + core) * LANE, LANE)

    def place(dx, dc):
        px, pc = lax.rem(x + dx, 4), lax.rem(core + dc, 2)
        return px * 2 + pc, (px * 4 + half * 2 + pc, fsdp)

    across = (x * 4 + (1 - half) * 2 + core, fsdp)

    barrier = pltpu.get_barrier_semaphore()
    for peer in PEERS:
        pl.semaphore_signal(barrier, inc=1, device_id=place(*peer)[1], device_id_type=MESH)
    pl.semaphore_signal(barrier, inc=1, device_id=across, device_id_type=MESH)

    small = [
        pltpu.make_async_copy(exponent, exponent_v, small_sem.at[0]),
        pltpu.make_async_copy(momentum, momentum_v, small_sem.at[1]),
    ]
    small[0].start()
    loads = []
    for k, first, tiles in spans():
        rows = pl.ds(first * TILE, tiles * TILE)
        pair = (
            pltpu.make_async_copy(inner.at[rows], inner_v.at[rows], load_sem.at[k, 0]),
            pltpu.make_async_copy(anchor.at[rows], anchor_v.at[rows], load_sem.at[k, 1]),
        )
        for copy in pair:
            copy.start()
        loads.append(pair)
    small[1].start()

    width = anchor.shape[1]
    blocks = width // BLOCK
    block_of = lax.broadcasted_iota(jnp.int32, (blocks, width), 1) // BLOCK
    row_of = lax.broadcasted_iota(jnp.int32, (blocks, width), 0)
    spread[...] = jnp.where(block_of == row_of, 1.0, 0.0).astype(jnp.bfloat16)
    small[0].wait()

    for k, first, tiles in spans():
        rows = pl.ds(first * TILE, tiles * TILE)
        powers = exponent_v[rows, :]
        scale, inverse = jnp.zeros(powers.shape, jnp.float32), jnp.zeros(powers.shape, jnp.float32)
        for power in (-1, 0, 1):
            scale = jnp.where(powers == power, jnp.float32(2.0**power), scale)
            inverse = jnp.where(powers == power, jnp.float32(2.0**-power), inverse)
        for value, target in ((scale, scale_v), (inverse, inverse_v)):
            target[rows, :] = jnp.dot(
                value.astype(jnp.bfloat16), spread[...], preferred_element_type=jnp.float32
            )
        for copy in loads[k]:
            copy.wait()

        def code(tile, carry):
            rows = pl.ds(pl.multiple_of(tile * TILE, TILE), TILE)
            for g in range(GROUP):
                for h in range(2):
                    columns = pl.ds(column_of(g, h), LANE)
                    delta = anchor_v[rows, columns].astype(jnp.float32) - inner_v[
                        rows, columns
                    ].astype(jnp.float32)
                    magnitude = jnp.abs(delta) * inverse_v[rows, columns]
                    scale = scale_v[rows, columns]
                    level = jnp.zeros(delta.shape, jnp.float32)
                    for bound, height in BOUNDS:
                        level = jnp.where(magnitude >= bound, jnp.float32(height), level)
                    level = level * jnp.where(delta < 0, -scale, scale)
                    coded[g, tile, h] = level.astype(jnp.bfloat16)
            return carry

        lax.fori_loop(first, first + tiles, code, 0)

    pl.semaphore_wait(barrier, len(PEERS) + 1)

    def start(source, destination, send, recv, device):
        pltpu.make_async_remote_copy(
            src_ref=source,
            dst_ref=destination,
            send_sem=send,
            recv_sem=recv,
            device_id=device,
            device_id_type=MESH,
        ).start()

    def wait(buffer, semaphore):
        pltpu.make_async_copy(buffer, buffer, semaphore).wait()

    for k, first, tiles in spans():
        span = pl.ds(first, tiles)
        for slot, peer in enumerate(PEERS):
            there, device = place(*peer)
            start(
                coded.at[there, span], arrived.at[slot, span], rs_send.at[k], rs_recv.at[k], device
            )

    small[1].wait()
    for k, first, tiles in spans():
        span = pl.ds(first, tiles)
        wait(arrived.at[:, span], rs_recv.at[k])

        def add(tile, carry):
            rows = pl.ds(pl.multiple_of(tile * TILE, TILE), TILE)
            own = coded[group, tile, half].astype(jnp.float32)
            other = coded[group, tile, 1 - half].astype(jnp.float32)
            for slot in range(len(PEERS)):
                own = own + arrived[slot, tile, half].astype(jnp.float32)
                other = other + arrived[slot, tile, 1 - half].astype(jnp.float32)
            anchor_own = anchor_v[rows, pl.ds(own_column, LANE)].astype(jnp.float32)
            mine = MINE * anchor_own - OTHER * own - (0.7 * 0.81) * momentum_v[rows, :]
            own_sum[rows, :] = own
            z_out[tile, 0] = mine.astype(jnp.bfloat16)
            z_out[tile, 1] = other.astype(jnp.bfloat16)
            return carry

        lax.fori_loop(first, first + tiles, add, 0)
        start(z_out.at[span], z_in.at[span], z_send.at[k], z_recv.at[k], across)

    for k, first, tiles in spans():
        span = pl.ds(first, tiles)
        wait(z_in.at[span], z_recv.at[k])

        def update(tile, carry):
            rows = pl.ds(pl.multiple_of(tile * TILE, TILE), TILE)

            def new(column, part, sums):
                wide = anchor_v[rows, pl.ds(column, LANE)].astype(jnp.float32)
                rest = (1.0 - MINE) * wide - OTHER * sums.astype(jnp.float32)
                return (part.astype(jnp.float32) + rest).astype(jnp.bfloat16)

            theirs = z_in[tile, 1]
            gathered[group, tile, half] = new(own_column, z_out[tile, 0], theirs)
            gathered[group, tile, 1 - half] = new(other_column, z_in[tile, 0], z_out[tile, 1])
            outer_grad = (own_sum[rows, :] + theirs.astype(jnp.float32)) * (1.0 / REPS)
            momentum_next[rows, :] = 0.9 * momentum_v[rows, :] + outer_grad
            return carry

        lax.fori_loop(first, first + tiles, update, 0)
        for slot, peer in enumerate(PEERS):
            _, device = place(*peer)
            piece = gathered.at[group, span]
            start(piece, piece, ag_send.at[k], ag_recv.at[k], device)

    for k, first, tiles in spans():
        span = pl.ds(first, tiles)
        wait(arrived.at[:, span], rs_send.at[k])
        wait(z_out.at[span], z_send.at[k])
    for k, first, tiles in spans():
        span = pl.ds(first, tiles)
        wait(arrived.at[:, span], ag_recv.at[k])
        wait(arrived.at[:, span], ag_send.at[k])


def mix(inner, gathered, momentum_in, mixed, new_anchor, momentum_out):
    for t in range(gathered.shape[1]):
        rows = pl.ds(t * TILE, TILE)
        for g in range(GROUP):
            for h in range(2):
                columns = pl.ds(column_of(g, h), LANE)
                new = gathered[g, t, h]
                new_anchor[rows, columns] = new
                mixed[rows, columns] = (
                    0.5 * inner[rows, columns].astype(jnp.float32) + 0.5 * new.astype(jnp.float32)
                ).astype(jnp.bfloat16)
    momentum_out[...] = momentum_in[...]


def on_device(inner, anchor, exponent, momentum):
    rows, width = anchor.shape[1:]
    tiles = rows // TILE
    blocks = exponent.shape[-1]
    inner2 = inner.reshape(rows, width)
    chunks = len(CHUNKS)
    anywhere = pl.BlockSpec(memory_space=pl.ANY)
    inside = pl.BlockSpec(memory_space=pltpu.VMEM)
    dma = pltpu.SemaphoreType.DMA
    gathered, momentum_next = pl.pallas_call(
        exchange,
        out_shape=(
            jax.ShapeDtypeStruct((GROUP, tiles, 2, TILE, LANE), jnp.bfloat16),
            jax.ShapeDtypeStruct((rows, LANE), jnp.float32),
        ),
        in_specs=[anywhere] * 4,
        out_specs=(inside, inside),
        scratch_shapes=[
            pltpu.VMEM((rows, width), jnp.bfloat16),
            pltpu.VMEM((rows, width), jnp.bfloat16),
            pltpu.VMEM((rows, blocks), jnp.int32),
            pltpu.VMEM((blocks, width), jnp.bfloat16),
            pltpu.VMEM((rows, width), jnp.float32),
            pltpu.VMEM((rows, width), jnp.float32),
            pltpu.VMEM((GROUP, tiles, 2, TILE, LANE), jnp.bfloat16),
            pltpu.VMEM((len(PEERS), tiles, 2, TILE, LANE), jnp.bfloat16),
            pltpu.VMEM((rows, LANE), jnp.float32),
            pltpu.VMEM((tiles, 2, TILE, LANE), jnp.bfloat16),
            pltpu.VMEM((tiles, 2, TILE, LANE), jnp.bfloat16),
            dma((chunks, 2)),
            dma((2,)),
            dma((chunks,)),
            dma((chunks,)),
            dma((chunks,)),
            dma((chunks,)),
            dma((chunks,)),
            dma((chunks,)),
            pltpu.VMEM((rows, LANE), jnp.float32),
        ],
        compiler_params=pltpu.CompilerParams(
            collective_id=0, has_side_effects=True, vmem_limit_bytes=24 << 20
        ),
        name="exchange",
    )(
        inner2,
        anchor.reshape(rows, width),
        exponent.reshape(rows, blocks),
        momentum.reshape(rows, LANE),
    )

    steps = 4
    part = rows // steps
    wide = pl.BlockSpec((part, width), lambda i: (i, 0))
    narrow = pl.BlockSpec((part, LANE), lambda i: (i, 0))
    mixed, new_anchor, momentum_next = pl.pallas_call(
        mix,
        out_shape=(
            jax.ShapeDtypeStruct((rows, width), jnp.bfloat16),
            jax.ShapeDtypeStruct((rows, width), jnp.bfloat16),
            jax.ShapeDtypeStruct((rows, LANE), jnp.float32),
        ),
        grid=(steps,),
        in_specs=[
            wide,
            pl.BlockSpec((GROUP, part // TILE, 2, TILE, LANE), lambda i: (0, i, 0, 0, 0)),
            narrow,
        ],
        out_specs=(wide, wide, narrow),
        compiler_params=pltpu.CompilerParams(vmem_limit_bytes=16 << 20),
        name="mix",
    )(inner2, gathered, momentum_next)
    return (
        mixed.reshape(inner.shape),
        new_anchor.reshape(anchor.shape),
        momentum_next.reshape(momentum.shape),
    )


def solution(mesh):
    return jax.shard_map(
        on_device,
        mesh=mesh,
        in_specs=(
            P("rep", None, "fsdp", None),
            P(None, "fsdp", None),
            P("rep", None, "fsdp", None),
            P(None, "fsdp", "rep"),
        ),
        out_specs=(P("rep", None, "fsdp", None), P(None, "fsdp", None), P(None, "fsdp", "rep")),
        check_vma=False,
    )
```

time: 211 us -> 50.4 us (0.24)
  waiting for transfers between devices: 183 us -> 0 us
  Pallas kernels: 0 us -> 46.1 us
  between operations: 14.1 us -> 0.67 us
  other arithmetic: 7.75 us -> 0 us
  local copies, waits for them, and re-layouts: 5.79 us -> 3.41 us
    reduce_scatter x1 -> x0, waiting for transfers between devices: 111 us -> none  [on_device(): lax.psum_scatter(coded.astype(jnp.float32).astype(jnp.bfloat16), 'rep', s...]
    all_gather x1 -> x0, waiting for transfers between devices: 72.4 us -> none  [on_device(): new_anchor = lax.all_gather(shard_new, 'rep', axis=2, tiled=True)]
    pallas_call x0 -> x2, Pallas kernels: none -> 46.1 us  [the longest x1 44 us: on_device(): pl.pallas_call(exchange, out_shape=(jax.ShapeDtypeStruct((GROUP, tiles, 2...]
    convert_element_type x3 -> x0, other arithmetic: 6.11 us -> none  [the longest x1 2.99 us: encode(): return signed.reshape(shape).astype(jnp.bfloat16)]
    unnamed x14 -> x7, local copies, waits for them, and re-layouts: 5.79 us -> 3.41 us
  transfers between devices with their start and end apart: 2 -> 0, of which waited for: 2 -> 0; matrix products, arithmetic and copies ran while one was open for 1% -> 0% of each run, Pallas kernels for 0% -> 0%
where the time goes in v1:
time: 50.4 us; the launch traced here: 50.1 us
  Pallas kernels  46.1 us (91%)
  local copies, waits for them, and re-layouts  3.41 us (7%)
  between operations  0.67 us (1%)
    pallas_call x1, Pallas kernels, on_device(): pl.pallas_call(exchange, out_shape=(jax.ShapeDtypeStruct((GROUP, tiles, 2...  44 us
    unnamed x7, local copies, waits for them, and re-layouts  3.41 us
    pallas_call x1, Pallas kernels, on_device(): pl.pallas_call(mix, out_shape=(jax.ShapeDtypeStruct((rows, width), jnp.bf...  2.03 us

profile of v1, /device:TPU:1, one launch (start us, length us, event | category | flops | bytes accessed | tf_op | source)
XLA Modules:
  0.0 50.1 jit_solution(2615484096806030630)
XLA Ops:
  0.6 0.0 copy-start.2
  0.6 1.0 %copy.7 = s32[1,1,256,64]{3,2,1,0:T(8,128)S(1)} copy(s32[1,1,256,64]{2,3,1,0:T(8,128)} %param.6) | data formatting | bytes 131072 | tf_op args[2]
  1.6 0.0 copy-done.2
  1.6 0.0 copy-start
  1.6 1.2 %copy-done = bf16[1,1,256,2048]{3,2,1,0:T(8,128)(2,1)S(1)} copy-done((bf16[1,1,256,2048]{3,2,1,0:T(8,128)(2,1)S(1)}, bf16[1,1,256,2048]{3,2,1,0:T(8,128)(2,1)}, u32[]{:S(2)}) %copy-start) | copy-done | bytes 1048600
  2.8 0.0 copy-start.1
  2.9 1.2 %copy-done.1 = bf16[1,256,2048]{2,1,0:T(8,128)(2,1)S(1)} copy-done((bf16[1,256,2048]{2,1,0:T(8,128)(2,1)S(1)}, bf16[1,256,2048]{2,1,0:T(8,128)(2,1)}, u32[]{:S(2)}) %copy-start.1) | copy-done | bytes 1048600
  4.1 44.0 %exchange.1 = (bf16[8,16,2,16,128]{4,3,2,1,0:T(8,128)(2,1)S(1)}, f32[256,128]{1,0:T(8,128)S(1)}) custom-call(bf16[256,2048]{1,0:T(8,128)(2,1)S(1)} %bitcast.7, bf16[256,2048]{1,0:T(8,128)(2,1)S(1)} %bitcast.9, s32[256,64]{1,0:T(8,128)S(1)} %bitcast.10, f32[256,128]{1,0:T(8,128)S(1)} %bitcast.11), custom_call_target="tpu_custom_call" | custom-call | tf_op jit(solution)/shard_map/exchange/pallas_call | solution.py:238
  48.1 2.0 %mix.1 = (bf16[256,2048]{1,0:T(8,128)(2,1)}, bf16[256,2048]{1,0:T(8,128)(2,1)}, f32[256,128]{1,0:T(8,128)}) custom-call(bf16[256,2048]{1,0:T(8,128)(2,1)S(1)} %bitcast.8, bf16[8,16,2,16,128]{4,3,2,1,0:T(8,128)(2,1)S(1)} %get-tuple-element.8.gathered, f32[256,128]{1,0:T(8,128)S(1)} %get-tuple-element.9.momentum_in), custom_call_target="tpu_custom_call" | custom-call | tf_op jit(solution)/shard_map/mix/pallas_call | solution.py:283
Async XLA Ops:
  0.6 1.0 %copy-start.2 = (f32[1,256,128]{2,1,0:T(8,128)S(1)}, f32[1,256,128]{2,1,0:T(8,128)}, u32[]{:S(2)}) copy-start(f32[1,256,128]{2,1,0:T(8,128)} %param.7) | copy-start | bytes 393220
  1.6 1.2 %copy-start = (bf16[1,1,256,2048]{3,2,1,0:T(8,128)(2,1)S(1)}, bf16[1,1,256,2048]{3,2,1,0:T(8,128)(2,1)}, u32[]{:S(2)}) copy-start(bf16[1,1,256,2048]{3,2,1,0:T(8,128)(2,1)} %param.4) | copy-start | bytes 3145732
  2.8 1.2 %copy-start.1 = (bf16[1,256,2048]{2,1,0:T(8,128)(2,1)S(1)}, bf16[1,256,2048]{2,1,0:T(8,128)(2,1)}, u32[]{:S(2)}) copy-start(bf16[1,256,2048]{2,1,0:T(8,128)(2,1)} %param.5) | copy-start | bytes 3145732

commit v2 on v1

--- a/solution.py
+++ b/solution.py
@@ -40,6 +40,7 @@
     inner_v,
     anchor_v,
     exponent_v,
+    power_rows,
     spread,
     scale_v,
     inverse_v,
@@ -57,6 +58,8 @@
     ag_send,
     ag_recv,
     momentum_v,
+    near_sem,
+    far_sem,
 ):
     rep, fsdp = lax.axis_index("rep"), lax.axis_index("fsdp")
     x, half, core = rep // 4, (rep // 2) % 2, rep % 2
@@ -70,10 +73,19 @@
 
     across = (x * 4 + (1 - half) * 2 + core, fsdp)
 
+    partner = (x * 4 + half * 2 + 1 - core, fsdp)
+
     barrier = pltpu.get_barrier_semaphore()
-    for peer in PEERS:
-        pl.semaphore_signal(barrier, inc=1, device_id=place(*peer)[1], device_id_type=MESH)
-    pl.semaphore_signal(barrier, inc=1, device_id=across, device_id_type=MESH)
+    for dx in range(1, 4):
+        hub = (lax.rem(x + dx, 4) * 4 + half * 2, fsdp)
+        pl.semaphore_signal(barrier, inc=1, device_id=hub, device_id_type=MESH)
+
+    @pl.when(core == 1)
+    def _():
+        pl.semaphore_signal(barrier, inc=1, device_id=partner, device_id_type=MESH)
+
+    far = (x * 4 + (1 - half) * 2 + 1, fsdp)
+    pl.semaphore_signal(barrier, inc=1, device_id=far, device_id_type=MESH)
 
     small = [
         pltpu.make_async_copy(exponent, exponent_v, small_sem.at[0]),
@@ -98,10 +110,24 @@
     row_of = lax.broadcasted_iota(jnp.int32, (blocks, width), 0)
     spread[...] = jnp.where(block_of == row_of, 1.0, 0.0).astype(jnp.bfloat16)
     small[0].wait()
+    power_rows[...] = exponent_v[...].T
+
+    def start(source, destination, send, recv, device):
+        pltpu.make_async_remote_copy(
+            src_ref=source,
+            dst_ref=destination,
+            send_sem=send,
+            recv_sem=recv,
+            device_id=device,
+            device_id_type=MESH,
+        ).start()
+
+    def wait(buffer, semaphore):
+        pltpu.make_async_copy(buffer, buffer, semaphore).wait()
 
     for k, first, tiles in spans():
         rows = pl.ds(first * TILE, tiles * TILE)
-        powers = exponent_v[rows, :]
+        powers = power_rows[rows, :]
         scale, inverse = jnp.zeros(powers.shape, jnp.float32), jnp.zeros(powers.shape, jnp.float32)
         for power in (-1, 0, 1):
             scale = jnp.where(powers == power, jnp.float32(2.0**power), scale)
@@ -132,28 +158,32 @@
 
         lax.fori_loop(first, first + tiles, code, 0)
 
-    pl.semaphore_wait(barrier, len(PEERS) + 1)
-
-    def start(source, destination, send, recv, device):
-        pltpu.make_async_remote_copy(
-            src_ref=source,
-            dst_ref=destination,
-            send_sem=send,
-            recv_sem=recv,
-            device_id=device,
-            device_id_type=MESH,
-        ).start()
-
-    def wait(buffer, semaphore):
-        pltpu.make_async_copy(buffer, buffer, semaphore).wait()
-
-    for k, first, tiles in spans():
+        if k == 0:
+
+            @pl.when(core == 0)
+            def _():
+                pl.semaphore_wait(barrier, len(PEERS))
+                pl.semaphore_signal(near_sem, inc=1, device_id=partner, device_id_type=MESH)
+
+            @pl.when(core == 1)
+            def _():
+                pl.semaphore_wait(near_sem, 1)
+
         span = pl.ds(first, tiles)
         for slot, peer in enumerate(PEERS):
             there, device = place(*peer)
             start(
                 coded.at[there, span], arrived.at[slot, span], rs_send.at[k], rs_recv.at[k], device
             )
+
+    @pl.when(core == 1)
+    def _():
+        pl.semaphore_wait(barrier, 2)
+        pl.semaphore_signal(far_sem, inc=1, device_id=partner, device_id_type=MESH)
+
+    @pl.when(core == 0)
+    def _():
+        pl.semaphore_wait(far_sem, 1)
 
     small[1].wait()
     for k, first, tiles in spans():
@@ -232,7 +262,7 @@
     blocks = exponent.shape[-1]
     inner2 = inner.reshape(rows, width)
     chunks = len(CHUNKS)
-    anywhere = pl.BlockSpec(memory_space=pl.ANY)
+    outside = pl.BlockSpec(memory_space=pltpu.HBM)
     inside = pl.BlockSpec(memory_space=pltpu.VMEM)
     dma = pltpu.SemaphoreType.DMA
     gathered, momentum_next = pl.pallas_call(
@@ -241,11 +271,12 @@
             jax.ShapeDtypeStruct((GROUP, tiles, 2, TILE, LANE), jnp.bfloat16),
             jax.ShapeDtypeStruct((rows, LANE), jnp.float32),
         ),
-        in_specs=[anywhere] * 4,
+        in_specs=[outside] * 4,
         out_specs=(inside, inside),
         scratch_shapes=[
             pltpu.VMEM((rows, width), jnp.bfloat16),
             pltpu.VMEM((rows, width), jnp.bfloat16),
+            pltpu.VMEM((blocks, rows), jnp.int32),
             pltpu.VMEM((rows, blocks), jnp.int32),
             pltpu.VMEM((blocks, width), jnp.bfloat16),
             pltpu.VMEM((rows, width), jnp.float32),
@@ -264,16 +295,23 @@
             dma((chunks,)),
             dma((chunks,)),
             pltpu.VMEM((rows, LANE), jnp.float32),
+            pltpu.SemaphoreType.REGULAR,
+            pltpu.SemaphoreType.REGULAR,
         ],
         compiler_params=pltpu.CompilerParams(
             collective_id=0, has_side_effects=True, vmem_limit_bytes=24 << 20
         ),
         name="exchange",
     )(
-        inner2,
-        anchor.reshape(rows, width),
-        exponent.reshape(rows, blocks),
-        momentum.reshape(rows, LANE),
+        *(
+            pltpu.with_memory_space_constraint(array, pltpu.HBM)
+            for array in (
+                inner2,
+                anchor.reshape(rows, width),
+                exponent.reshape(rows, blocks).T,
+                momentum.reshape(rows, LANE),
+            )
+        )
     )
 
     steps = 4

time: 50.4 us -> 47.9 us (0.950)
  the two profiles are of different devices: /device:TPU:1 before, /device:TPU:9 now
where the time goes in v2:
time: 47.9 us; the launch traced here: 47.8 us
  Pallas kernels  47.1 us (98%)
  between operations  0.65 us (1%)
    pallas_call x1, Pallas kernels, on_device(): pl.pallas_call(exchange, out_shape=(jax.ShapeDtypeStruct((GROUP, tiles, 2...  45.1 us
    pallas_call x1, Pallas kernels, on_device(): pl.pallas_call(mix, out_shape=(jax.ShapeDtypeStruct((rows, width), jnp.bf...  2.03 us

profile of v2, /device:TPU:9, one launch (start us, length us, event | category | flops | bytes accessed | tf_op | source)
XLA Modules:
  0.0 47.8 jit_solution(9505919738485783987)
XLA Ops:
  0.6 0.0 copy-start
  0.6 45.1 %exchange.1 = (bf16[8,16,2,16,128]{4,3,2,1,0:T(8,128)(2,1)S(1)}, f32[256,128]{1,0:T(8,128)S(1)}) custom-call(bf16[256,2048]{1,0:T(8,128)(2,1)} %bitcast.9, bf16[256,2048]{1,0:T(8,128)(2,1)} %bitcast.11, s32[64,256]{1,0:T(8,128)} %bitcast.13, f32[256,128]{1,0:T(8,128)} %bitcast.12), custom_call_target="tpu_custom_call" | custom-call | tf_op jit(solution)/shard_map/exchange/pallas_call | solution.py:268
  45.7 0.0 copy-done
  45.8 2.0 %mix.1 = (bf16[256,2048]{1,0:T(8,128)(2,1)}, bf16[256,2048]{1,0:T(8,128)(2,1)}, f32[256,128]{1,0:T(8,128)}) custom-call(bf16[256,2048]{1,0:T(8,128)(2,1)S(1)} %bitcast.10, bf16[8,16,2,16,128]{4,3,2,1,0:T(8,128)(2,1)S(1)} %get-tuple-element.8.gathered, f32[256,128]{1,0:T(8,128)S(1)} %get-tuple-element.9.momentum_in), custom_call_target="tpu_custom_call" | custom-call | tf_op jit(solution)/shard_map/mix/pallas_call | solution.py:321
Async XLA Ops:
  0.6 45.1 %copy-start = (bf16[1,1,256,2048]{3,2,1,0:T(8,128)(2,1)S(1)}, bf16[1,1,256,2048]{3,2,1,0:T(8,128)(2,1)}, u32[]{:S(2)}) copy-start(bf16[1,1,256,2048]{3,2,1,0:T(8,128)(2,1)} %param.4) | copy-start | bytes 3145732

commit v3 on v2

--- a/solution.py
+++ b/solution.py
@@ -11,23 +11,20 @@
 BLOCK = 32
 LANE = 128
 TILE = 16
-GROUP = 8
+XS = 4
 REPS = 16
 MINE, OTHER = 0.5, 0.7 * 1.9 / REPS
 BOUNDS = ((0.25, 0.5), (0.75, 1.0), (1.25, 1.5), (1.75, 2.0), (2.5, 3.0), (3.5, 4.0), (5.0, 6.0))
 CHUNKS = (4, 4, 4, 4)
-PEERS = tuple((dx, dc) for dx in range(4) for dc in range(2) if (dx, dc) != (0, 0))
-
-
-def column_of(group, half):
-    return ((group // 2) * 4 + half * 2 + group % 2) * LANE
-
-
-def spans():
-    first = 0
-    for k, tiles in enumerate(CHUNKS):
-        yield k, first, tiles
-        first += tiles
+PLACES = tuple((c, x, h) for c in range(2) for x in range(XS) for h in range(2))
+HEARD = 2 * XS - 1
+
+
+def column_of(core, x, half):
+    return (x * 4 + half * 2 + core) * LANE
+
+
+SPANS = tuple((k, sum(CHUNKS[:k]), tiles) for k, tiles in enumerate(CHUNKS))
 
 
 def exchange(
@@ -45,31 +42,36 @@
     scale_v,
     inverse_v,
     coded,
+    pair_in,
+    pairs,
     arrived,
     own_sum,
     z_out,
     z_in,
     load_sem,
     small_sem,
+    core_send,
+    core_recv,
     rs_send,
     rs_recv,
     z_send,
     z_recv,
     ag_send,
     ag_recv,
+    out_send,
+    out_recv,
     momentum_v,
     near_sem,
     far_sem,
 ):
     rep, fsdp = lax.axis_index("rep"), lax.axis_index("fsdp")
     x, half, core = rep // 4, (rep // 2) % 2, rep % 2
-    group = x * 2 + core
     own_column = pl.multiple_of(rep * LANE, LANE)
     other_column = pl.multiple_of((x * 4 + (1 - half) * 2 + core) * LANE, LANE)
 
-    def place(dx, dc):
-        px, pc = lax.rem(x + dx, 4), lax.rem(core + dc, 2)
-        return px * 2 + pc, (px * 4 + half * 2 + pc, fsdp)
+    def beside(dx):
+        there = lax.rem(x + dx, XS)
+        return there, (there * 4 + half * 2 + core, fsdp)
 
     across = (x * 4 + (1 - half) * 2 + core, fsdp)
 
@@ -93,7 +95,7 @@
     ]
     small[0].start()
     loads = []
-    for k, first, tiles in spans():
+    for k, first, tiles in SPANS:
         rows = pl.ds(first * TILE, tiles * TILE)
         pair = (
             pltpu.make_async_copy(inner.at[rows], inner_v.at[rows], load_sem.at[k, 0]),
@@ -125,7 +127,26 @@
     def wait(buffer, semaphore):
         pltpu.make_async_copy(buffer, buffer, semaphore).wait()
 
-    for k, first, tiles in spans():
+    def pass_pairs(k):
+        _, first, tiles = SPANS[k]
+        span = pl.ds(first, tiles)
+        wait(pair_in.at[:, span], core_recv.at[k])
+
+        def add(tile, carry):
+            for place in range(XS):
+                for h in range(2):
+                    pairs[place, tile, h] = (
+                        coded[core, place, tile, h].astype(jnp.float32)
+                        + pair_in[place, tile, h].astype(jnp.float32)
+                    ).astype(jnp.bfloat16)
+            return carry
+
+        lax.fori_loop(first, first + tiles, add, 0)
+        for slot in range(XS - 1):
+            there, device = beside(slot + 1)
+            start(pairs.at[there, span], arrived.at[slot, span], rs_send.at[k], rs_recv.at[k], device)
+
+    for k, first, tiles in SPANS:
         rows = pl.ds(first * TILE, tiles * TILE)
         powers = power_rows[rows, :]
         scale, inverse = jnp.zeros(powers.shape, jnp.float32), jnp.zeros(powers.shape, jnp.float32)
@@ -141,19 +162,18 @@
 
         def code(tile, carry):
             rows = pl.ds(pl.multiple_of(tile * TILE, TILE), TILE)
-            for g in range(GROUP):
-                for h in range(2):
-                    columns = pl.ds(column_of(g, h), LANE)
-                    delta = anchor_v[rows, columns].astype(jnp.float32) - inner_v[
-                        rows, columns
-                    ].astype(jnp.float32)
-                    magnitude = jnp.abs(delta) * inverse_v[rows, columns]
-                    scale = scale_v[rows, columns]
-                    level = jnp.zeros(delta.shape, jnp.float32)
-                    for bound, height in BOUNDS:
-                        level = jnp.where(magnitude >= bound, jnp.float32(height), level)
-                    level = level * jnp.where(delta < 0, -scale, scale)
-                    coded[g, tile, h] = level.astype(jnp.bfloat16)
+            for c, place, h in PLACES:
+                columns = pl.ds(column_of(c, place, h), LANE)
+                delta = anchor_v[rows, columns].astype(jnp.float32) - inner_v[
+                    rows, columns
+                ].astype(jnp.float32)
+                magnitude = jnp.abs(delta) * inverse_v[rows, columns]
+                scale = scale_v[rows, columns]
+                level = jnp.zeros(delta.shape, jnp.float32)
+                for bound, height in BOUNDS:
+                    level = jnp.where(magnitude >= bound, jnp.float32(height), level)
+                level = level * jnp.where(delta < 0, -scale, scale)
+                coded[c, place, tile, h] = level.astype(jnp.bfloat16)
             return carry
 
         lax.fori_loop(first, first + tiles, code, 0)
@@ -162,7 +182,7 @@
 
             @pl.when(core == 0)
             def _():
-                pl.semaphore_wait(barrier, len(PEERS))
+                pl.semaphore_wait(barrier, HEARD)
                 pl.semaphore_signal(near_sem, inc=1, device_id=partner, device_id_type=MESH)
 
             @pl.when(core == 1)
@@ -170,11 +190,12 @@
                 pl.semaphore_wait(near_sem, 1)
 
         span = pl.ds(first, tiles)
-        for slot, peer in enumerate(PEERS):
-            there, device = place(*peer)
-            start(
-                coded.at[there, span], arrived.at[slot, span], rs_send.at[k], rs_recv.at[k], device
-            )
+        start(
+            coded.at[1 - core, :, span], pair_in.at[:, span], core_send.at[k], core_recv.at[k], partner
+        )
+        if k > 0:
+            pass_pairs(k - 1)
+    pass_pairs(len(CHUNKS) - 1)
 
     @pl.when(core == 1)
     def _():
@@ -186,15 +207,15 @@
         pl.semaphore_wait(far_sem, 1)
 
     small[1].wait()
-    for k, first, tiles in spans():
+    for k, first, tiles in SPANS:
         span = pl.ds(first, tiles)
         wait(arrived.at[:, span], rs_recv.at[k])
 
         def add(tile, carry):
             rows = pl.ds(pl.multiple_of(tile * TILE, TILE), TILE)
-            own = coded[group, tile, half].astype(jnp.float32)
-            other = coded[group, tile, 1 - half].astype(jnp.float32)
-            for slot in range(len(PEERS)):
+            own = pairs[x, tile, half].astype(jnp.float32)
+            other = pairs[x, tile, 1 - half].astype(jnp.float32)
+            for slot in range(XS - 1):
                 own = own + arrived[slot, tile, half].astype(jnp.float32)
                 other = other + arrived[slot, tile, 1 - half].astype(jnp.float32)
             anchor_own = anchor_v[rows, pl.ds(own_column, LANE)].astype(jnp.float32)
@@ -207,7 +228,14 @@
         lax.fori_loop(first, first + tiles, add, 0)
         start(z_out.at[span], z_in.at[span], z_send.at[k], z_recv.at[k], across)
 
-    for k, first, tiles in spans():
+    def hand_over(k):
+        _, first, tiles = SPANS[k]
+        span = pl.ds(first, tiles)
+        wait(arrived.at[:, span], ag_recv.at[k])
+        whole = gathered.at[core, :, span]
+        start(whole, whole, out_send.at[k], out_recv.at[k], partner)
+
+    for k, first, tiles in SPANS:
         span = pl.ds(first, tiles)
         wait(z_in.at[span], z_recv.at[k])
 
@@ -220,39 +248,41 @@
                 return (part.astype(jnp.float32) + rest).astype(jnp.bfloat16)
 
             theirs = z_in[tile, 1]
-            gathered[group, tile, half] = new(own_column, z_out[tile, 0], theirs)
-            gathered[group, tile, 1 - half] = new(other_column, z_in[tile, 0], z_out[tile, 1])
+            gathered[core, x, tile, half] = new(own_column, z_out[tile, 0], theirs)
+            gathered[core, x, tile, 1 - half] = new(other_column, z_in[tile, 0], z_out[tile, 1])
             outer_grad = (own_sum[rows, :] + theirs.astype(jnp.float32)) * (1.0 / REPS)
             momentum_next[rows, :] = 0.9 * momentum_v[rows, :] + outer_grad
             return carry
 
         lax.fori_loop(first, first + tiles, update, 0)
-        for slot, peer in enumerate(PEERS):
-            _, device = place(*peer)
-            piece = gathered.at[group, span]
-            start(piece, piece, ag_send.at[k], ag_recv.at[k], device)
-
-    for k, first, tiles in spans():
-        span = pl.ds(first, tiles)
+        piece = gathered.at[core, x, span]
+        for slot in range(XS - 1):
+            start(piece, piece, ag_send.at[k], ag_recv.at[k], beside(slot + 1)[1])
+        if k > 0:
+            hand_over(k - 1)
+    hand_over(len(CHUNKS) - 1)
+
+    for k, first, tiles in SPANS:
+        span = pl.ds(first, tiles)
+        wait(pair_in.at[:, span], core_send.at[k])
         wait(arrived.at[:, span], rs_send.at[k])
         wait(z_out.at[span], z_send.at[k])
-    for k, first, tiles in spans():
-        span = pl.ds(first, tiles)
-        wait(arrived.at[:, span], ag_recv.at[k])
         wait(arrived.at[:, span], ag_send.at[k])
+        wait(pair_in.at[:, span], out_send.at[k])
+    for k, first, tiles in SPANS:
+        wait(pair_in.at[:, pl.ds(first, tiles)], out_recv.at[k])
 
 
 def mix(inner, gathered, momentum_in, mixed, new_anchor, momentum_out):
-    for t in range(gathered.shape[1]):
+    for t in range(gathered.shape[2]):
         rows = pl.ds(t * TILE, TILE)
-        for g in range(GROUP):
-            for h in range(2):
-                columns = pl.ds(column_of(g, h), LANE)
-                new = gathered[g, t, h]
-                new_anchor[rows, columns] = new
-                mixed[rows, columns] = (
-                    0.5 * inner[rows, columns].astype(jnp.float32) + 0.5 * new.astype(jnp.float32)
-                ).astype(jnp.bfloat16)
+        for c, x, h in PLACES:
+            columns = pl.ds(column_of(c, x, h), LANE)
+            new = gathered[c, x, t, h]
+            new_anchor[rows, columns] = new
+            mixed[rows, columns] = (
+                0.5 * inner[rows, columns].astype(jnp.float32) + 0.5 * new.astype(jnp.float32)
+            ).astype(jnp.bfloat16)
     momentum_out[...] = momentum_in[...]
 
 
@@ -268,7 +298,7 @@
     gathered, momentum_next = pl.pallas_call(
         exchange,
         out_shape=(
-            jax.ShapeDtypeStruct((GROUP, tiles, 2, TILE, LANE), jnp.bfloat16),
+            jax.ShapeDtypeStruct((2, XS, tiles, 2, TILE, LANE), jnp.bfloat16),
             jax.ShapeDtypeStruct((rows, LANE), jnp.float32),
         ),
         in_specs=[outside] * 4,
@@ -281,19 +311,16 @@
             pltpu.VMEM((blocks, width), jnp.bfloat16),
             pltpu.VMEM((rows, width), jnp.float32),
             pltpu.VMEM((rows, width), jnp.float32),
-            pltpu.VMEM((GROUP, tiles, 2, TILE, LANE), jnp.bfloat16),
-            pltpu.VMEM((len(PEERS), tiles, 2, TILE, LANE), jnp.bfloat16),
+            pltpu.VMEM((2, XS, tiles, 2, TILE, LANE), jnp.bfloat16),
+            pltpu.VMEM((XS, tiles, 2, TILE, LANE), jnp.bfloat16),
+            pltpu.VMEM((XS, tiles, 2, TILE, LANE), jnp.bfloat16),
+            pltpu.VMEM((XS - 1, tiles, 2, TILE, LANE), jnp.bfloat16),
             pltpu.VMEM((rows, LANE), jnp.float32),
             pltpu.VMEM((tiles, 2, TILE, LANE), jnp.bfloat16),
             pltpu.VMEM((tiles, 2, TILE, LANE), jnp.bfloat16),
             dma((chunks, 2)),
             dma((2,)),
-            dma((chunks,)),
-            dma((chunks,)),
-            dma((chunks,)),
-            dma((chunks,)),
-            dma((chunks,)),
-            dma((chunks,)),
+            *[dma((chunks,))] * 10,
             pltpu.VMEM((rows, LANE), jnp.float32),
             pltpu.SemaphoreType.REGULAR,
             pltpu.SemaphoreType.REGULAR,
@@ -328,7 +355,7 @@
         grid=(steps,),
         in_specs=[
             wide,
-            pl.BlockSpec((GROUP, part // TILE, 2, TILE, LANE), lambda i: (0, i, 0, 0, 0)),
+            pl.BlockSpec((2, XS, part // TILE, 2, TILE, LANE), lambda i: (0, 0, i, 0, 0, 0)),
             narrow,
         ],
         out_specs=(wide, wide, narrow),

time: 47.9 us -> 45.8 us (0.956)
  the two profiles are of different devices: /device:TPU:9 before, /device:TPU:57 now
where the time goes in v3:
time: 45.8 us; the launch traced here: 45.7 us
  Pallas kernels  45 us (98%)
  between operations  0.65 us (1%)
    pallas_call x1, Pallas kernels, on_device(): pl.pallas_call(exchange, out_shape=(jax.ShapeDtypeStruct((2, XS, tiles, 2...  43 us
    pallas_call x1, Pallas kernels, on_device(): pl.pallas_call(mix, out_shape=(jax.ShapeDtypeStruct((rows, width), jnp.bf...  2.02 us

profile of v3, /device:TPU:57, one launch (start us, length us, event | category | flops | bytes accessed | tf_op | source)
XLA Modules:
  0.0 45.7 jit_solution(18280509803200548848)
XLA Ops:
  0.6 0.0 copy-start
  0.6 43.0 %exchange.1 = (bf16[2,4,16,2,16,128]{5,4,3,2,1,0:T(8,128)(2,1)S(1)}, f32[256,128]{1,0:T(8,128)S(1)}) custom-call(bf16[256,2048]{1,0:T(8,128)(2,1)} %bitcast.9, bf16[256,2048]{1,0:T(8,128)(2,1)} %bitcast.11, s32[64,256]{1,0:T(8,128)} %bitcast.13, f32[256,128]{1,0:T(8,128)} %bitcast.12), custom_call_target="tpu_custom_call" | custom-call | tf_op jit(solution)/shard_map/exchange/pallas_call | solution.py:298
  43.7 0.0 copy-done
  43.7 2.0 %mix.1 = (bf16[256,2048]{1,0:T(8,128)(2,1)}, bf16[256,2048]{1,0:T(8,128)(2,1)}, f32[256,128]{1,0:T(8,128)}) custom-call(bf16[256,2048]{1,0:T(8,128)(2,1)S(1)} %bitcast.10, bf16[2,4,16,2,16,128]{5,4,3,2,1,0:T(8,128)(2,1)S(1)} %get-tuple-element.8.gathered, f32[256,128]{1,0:T(8,128)S(1)} %get-tuple-element.9.momentum_in), custom_call_target="tpu_custom_call" | custom-call | tf_op jit(solution)/shard_map/mix/pallas_call | solution.py:348
Async XLA Ops:
  0.6 43.0 %copy-start = (bf16[1,1,256,2048]{3,2,1,0:T(8,128)(2,1)S(1)}, bf16[1,1,256,2048]{3,2,1,0:T(8,128)(2,1)}, u32[]{:S(2)}) copy-start(bf16[1,1,256,2048]{3,2,1,0:T(8,128)(2,1)} %param.4) | copy-start | bytes 3145732

commit v4 on v3

--- a/solution.py
+++ b/solution.py
@@ -15,7 +15,8 @@
 REPS = 16
 MINE, OTHER = 0.5, 0.7 * 1.9 / REPS
 BOUNDS = ((0.25, 0.5), (0.75, 1.0), (1.25, 1.5), (1.75, 2.0), (2.5, 3.0), (3.5, 4.0), (5.0, 6.0))
-CHUNKS = (4, 4, 4, 4)
+CHUNKS = (1, 2, 3, 4, 3, 2, 1)
+HOPS = len(CHUNKS) - 2
 PLACES = tuple((c, x, h) for c in range(2) for x in range(XS) for h in range(2))
 HEARD = 2 * XS - 1
 
@@ -24,6 +25,7 @@
     return (x * 4 + half * 2 + core) * LANE
 
 
+AHEAD = 2
 SPANS = tuple((k, sum(CHUNKS[:k]), tiles) for k, tiles in enumerate(CHUNKS))
 
 
@@ -32,8 +34,10 @@
     anchor,
     exponent,
     momentum,
+    mixed,
+    new_anchor,
+    momentum_next,
     gathered,
-    momentum_next,
     inner_v,
     anchor_v,
     exponent_v,
@@ -69,9 +73,9 @@
     own_column = pl.multiple_of(rep * LANE, LANE)
     other_column = pl.multiple_of((x * 4 + (1 - half) * 2 + core) * LANE, LANE)
 
-    def beside(dx):
+    def beside(dx, there_core):
         there = lax.rem(x + dx, XS)
-        return there, (there * 4 + half * 2 + core, fsdp)
+        return there, (there * 4 + half * 2 + there_core, fsdp)
 
     across = (x * 4 + (1 - half) * 2 + core, fsdp)
 
@@ -142,8 +146,8 @@
             return carry
 
         lax.fori_loop(first, first + tiles, add, 0)
-        for slot in range(XS - 1):
-            there, device = beside(slot + 1)
+        for slot in (1, 0, 2):
+            there, device = beside(slot + 1, core)
             start(pairs.at[there, span], arrived.at[slot, span], rs_send.at[k], rs_recv.at[k], device)
 
     for k, first, tiles in SPANS:
@@ -193,9 +197,10 @@
         start(
             coded.at[1 - core, :, span], pair_in.at[:, span], core_send.at[k], core_recv.at[k], partner
         )
-        if k > 0:
-            pass_pairs(k - 1)
-    pass_pairs(len(CHUNKS) - 1)
+        if k >= AHEAD:
+            pass_pairs(k - AHEAD)
+    for k in range(len(CHUNKS) - AHEAD, len(CHUNKS)):
+        pass_pairs(k)
 
     @pl.when(core == 1)
     def _():
@@ -235,6 +240,27 @@
         whole = gathered.at[core, :, span]
         start(whole, whole, out_send.at[k], out_recv.at[k], partner)
 
+    def mix(k):
+        _, first, tiles = SPANS[k]
+        span = pl.ds(first, tiles)
+        if k >= HOPS:
+            wait(arrived.at[:, span], ag_recv.at[k])
+        wait(pair_in.at[:, span], out_recv.at[k])
+
+        def part(tile, carry):
+            rows = pl.ds(pl.multiple_of(tile * TILE, TILE), TILE)
+            for c, place, h in PLACES:
+                columns = pl.ds(column_of(c, place, h), LANE)
+                new = gathered[c, place, tile, h]
+                new_anchor[rows, columns] = new
+                mixed[rows, columns] = (
+                    0.5 * inner_v[rows, columns].astype(jnp.float32)
+                    + 0.5 * new.astype(jnp.float32)
+                ).astype(jnp.bfloat16)
+            return carry
+
+        lax.fori_loop(first, first + tiles, part, 0)
+
     for k, first, tiles in SPANS:
         span = pl.ds(first, tiles)
         wait(z_in.at[span], z_recv.at[k])
@@ -256,11 +282,20 @@
 
         lax.fori_loop(first, first + tiles, update, 0)
         piece = gathered.at[core, x, span]
-        for slot in range(XS - 1):
-            start(piece, piece, ag_send.at[k], ag_recv.at[k], beside(slot + 1)[1])
-        if k > 0:
+        for slot in (1, 0, 2):
+            start(piece, piece, ag_send.at[k], ag_recv.at[k], beside(slot + 1, core)[1])
+        if k >= HOPS:
+            for slot in (1, 0, 2):
+                other_core = beside(slot + 1, 1 - core)[1]
+                start(piece, piece, out_send.at[k], out_recv.at[k], other_core)
+            start(piece, piece, out_send.at[k], out_recv.at[k], partner)
+        elif k > 0:
             hand_over(k - 1)
-    hand_over(len(CHUNKS) - 1)
+        if 2 <= k <= HOPS:
+            mix(k - 2)
+    hand_over(HOPS - 1)
+    for k in range(HOPS - 1, len(CHUNKS)):
+        mix(k)
 
     for k, first, tiles in SPANS:
         span = pl.ds(first, tiles)
@@ -269,21 +304,18 @@
         wait(z_out.at[span], z_send.at[k])
         wait(arrived.at[:, span], ag_send.at[k])
         wait(pair_in.at[:, span], out_send.at[k])
-    for k, first, tiles in SPANS:
-        wait(pair_in.at[:, pl.ds(first, tiles)], out_recv.at[k])
-
-
-def mix(inner, gathered, momentum_in, mixed, new_anchor, momentum_out):
-    for t in range(gathered.shape[2]):
-        rows = pl.ds(t * TILE, TILE)
-        for c, x, h in PLACES:
-            columns = pl.ds(column_of(c, x, h), LANE)
-            new = gathered[c, x, t, h]
-            new_anchor[rows, columns] = new
-            mixed[rows, columns] = (
-                0.5 * inner[rows, columns].astype(jnp.float32) + 0.5 * new.astype(jnp.float32)
-            ).astype(jnp.bfloat16)
-    momentum_out[...] = momentum_in[...]
+
+
+def flush(*refs):
+    results, outputs, sems = refs[:3], refs[3:6], refs[6]
+    copies = [
+        pltpu.make_async_copy(result, output, sems.at[i])
+        for i, (result, output) in enumerate(zip(results, outputs))
+    ]
+    for copy in copies:
+        copy.start()
+    for copy in copies:
+        copy.wait()
 
 
 def on_device(inner, anchor, exponent, momentum):
@@ -295,15 +327,18 @@
     outside = pl.BlockSpec(memory_space=pltpu.HBM)
     inside = pl.BlockSpec(memory_space=pltpu.VMEM)
     dma = pltpu.SemaphoreType.DMA
-    gathered, momentum_next = pl.pallas_call(
+    results = (
+        jax.ShapeDtypeStruct((rows, width), jnp.bfloat16),
+        jax.ShapeDtypeStruct((rows, width), jnp.bfloat16),
+        jax.ShapeDtypeStruct((rows, LANE), jnp.float32),
+    )
+    inside_results = pl.pallas_call(
         exchange,
-        out_shape=(
-            jax.ShapeDtypeStruct((2, XS, tiles, 2, TILE, LANE), jnp.bfloat16),
-            jax.ShapeDtypeStruct((rows, LANE), jnp.float32),
-        ),
+        out_shape=results,
         in_specs=[outside] * 4,
-        out_specs=(inside, inside),
+        out_specs=(inside,) * 3,
         scratch_shapes=[
+            pltpu.VMEM((2, XS, tiles, 2, TILE, LANE), jnp.bfloat16),
             pltpu.VMEM((rows, width), jnp.bfloat16),
             pltpu.VMEM((rows, width), jnp.bfloat16),
             pltpu.VMEM((blocks, rows), jnp.int32),
@@ -341,27 +376,16 @@
         )
     )
 
-    steps = 4
-    part = rows // steps
-    wide = pl.BlockSpec((part, width), lambda i: (i, 0))
-    narrow = pl.BlockSpec((part, LANE), lambda i: (i, 0))
+    anywhere = pl.BlockSpec(memory_space=pl.ANY)
     mixed, new_anchor, momentum_next = pl.pallas_call(
-        mix,
-        out_shape=(
-            jax.ShapeDtypeStruct((rows, width), jnp.bfloat16),
-            jax.ShapeDtypeStruct((rows, width), jnp.bfloat16),
-            jax.ShapeDtypeStruct((rows, LANE), jnp.float32),
-        ),
-        grid=(steps,),
-        in_specs=[
-            wide,
-            pl.BlockSpec((2, XS, part // TILE, 2, TILE, LANE), lambda i: (0, 0, i, 0, 0, 0)),
-            narrow,
-        ],
-        out_specs=(wide, wide, narrow),
+        flush,
+        out_shape=results,
+        in_specs=[anywhere] * 3,
+        out_specs=(anywhere,) * 3,
+        scratch_shapes=[dma((3,))],
         compiler_params=pltpu.CompilerParams(vmem_limit_bytes=16 << 20),
-        name="mix",
-    )(inner2, gathered, momentum_next)
+        name="flush",
+    )(*inside_results)
     return (
         mixed.reshape(inner.shape),
         new_anchor.reshape(anchor.shape),

time: 45.8 us -> 44.9 us (0.980)
  the two profiles are of different devices: /device:TPU:57 before, /device:TPU:1 now
where the time goes in v4:
time: 44.9 us; the launch traced here: 44.7 us
  Pallas kernels  44.1 us (98%)
  between operations  0.64 us (1%)
    pallas_call x1, Pallas kernels, on_device(): pl.pallas_call(exchange, out_shape=results, in_specs=[outside] * 4, out_s...  42.7 us
    pallas_call x1, Pallas kernels, on_device(): pl.pallas_call(flush, out_shape=results, in_specs=[anywhere] * 3, out_spe...  1.37 us

profile of v4, /device:TPU:1, one launch (start us, length us, event | category | flops | bytes accessed | tf_op | source)
XLA Modules:
  0.0 44.7 jit_solution(14343899845980016966)
XLA Ops:
  0.6 42.7 %exchange.1 = (bf16[256,2048]{1,0:T(8,128)(2,1)S(1)}, bf16[256,2048]{1,0:T(8,128)(2,1)S(1)}, f32[256,128]{1,0:T(8,128)S(1)}) custom-call(bf16[256,2048]{1,0:T(8,128)(2,1)} %bitcast.9, bf16[256,2048]{1,0:T(8,128)(2,1)} %bitcast.10, s32[64,256]{1,0:T(8,128)} %bitcast.12, f32[256,128]{1,0:T(8,128)} %bitcast.11), custom_call_target="tpu_custom_call" | custom-call | tf_op jit(solution)/shard_map/exchange/pallas_call | solution.py:335
  43.4 1.4 %flush.1 = (bf16[256,2048]{1,0:T(8,128)(2,1)}, bf16[256,2048]{1,0:T(8,128)(2,1)}, f32[256,128]{1,0:T(8,128)}) custom-call(bf16[256,2048]{1,0:T(8,128)(2,1)S(1)} %get-tuple-element.9.refs_0_, bf16[256,2048]{1,0:T(8,128)(2,1)S(1)} %get-tuple-element.10.refs_1_, f32[256,128]{1,0:T(8,128)S(1)} %get-tuple-element.11.refs_2_), custom_call_target="tpu_custom_call" | custom-call | tf_op jit(solution)/shard_map/flush/pallas_call | solution.py:380

commit v5 on v4

--- a/solution.py
+++ b/solution.py
@@ -231,6 +231,11 @@
             return carry
 
         lax.fori_loop(first, first + tiles, add, 0)
+
+        @pl.when(half == 1)
+        def _():
+            wait(z_in.at[span], z_recv.at[k])
+
         start(z_out.at[span], z_in.at[span], z_send.at[k], z_recv.at[k], across)
 
     def hand_over(k):
@@ -263,7 +268,10 @@
 
     for k, first, tiles in SPANS:
         span = pl.ds(first, tiles)
-        wait(z_in.at[span], z_recv.at[k])
+
+        @pl.when(half == 0)
+        def _():
+            wait(z_in.at[span], z_recv.at[k])
 
         def update(tile, carry):
             rows = pl.ds(pl.multiple_of(tile * TILE, TILE), TILE)
@@ -289,12 +297,9 @@
                 other_core = beside(slot + 1, 1 - core)[1]
                 start(piece, piece, out_send.at[k], out_recv.at[k], other_core)
             start(piece, piece, out_send.at[k], out_recv.at[k], partner)
-        elif k > 0:
-            hand_over(k - 1)
-        if 2 <= k <= HOPS:
-            mix(k - 2)
-    hand_over(HOPS - 1)
-    for k in range(HOPS - 1, len(CHUNKS)):
+    for k in range(HOPS):
+        hand_over(k)
+    for k in range(len(CHUNKS)):
         mix(k)
 
     for k, first, tiles in SPANS:

time: 44.9 us -> 52.4 us (1.17)
  the two profiles are of different devices: /device:TPU:1 before, /device:TPU:41 now
where the time goes in v5:
time: 52.4 us; the launch traced here: 52.3 us
  Pallas kernels  51.6 us (98%)
  between operations  0.64 us (1%)
    pallas_call x1, Pallas kernels, on_device(): pl.pallas_call(exchange, out_shape=results, in_specs=[outside] * 4, out_s...  50.2 us
    pallas_call x1, Pallas kernels, on_device(): pl.pallas_call(flush, out_shape=results, in_specs=[anywhere] * 3, out_spe...  1.37 us

profile of v5, /device:TPU:41, one launch (start us, length us, event | category | flops | bytes accessed | tf_op | source)
XLA Modules:
  0.0 52.3 jit_solution(2748929873015305763)
XLA Ops:
  0.6 50.2 %exchange.1 = (bf16[256,2048]{1,0:T(8,128)(2,1)S(1)}, bf16[256,2048]{1,0:T(8,128)(2,1)S(1)}, f32[256,128]{1,0:T(8,128)S(1)}) custom-call(bf16[256,2048]{1,0:T(8,128)(2,1)} %bitcast.9, bf16[256,2048]{1,0:T(8,128)(2,1)} %bitcast.10, s32[64,256]{1,0:T(8,128)} %bitcast.12, f32[256,128]{1,0:T(8,128)} %bitcast.11), custom_call_target="tpu_custom_call" | custom-call | tf_op jit(solution)/shard_map/exchange/pallas_call | solution.py:340
  50.9 1.4 %flush.1 = (bf16[256,2048]{1,0:T(8,128)(2,1)}, bf16[256,2048]{1,0:T(8,128)(2,1)}, f32[256,128]{1,0:T(8,128)}) custom-call(bf16[256,2048]{1,0:T(8,128)(2,1)S(1)} %get-tuple-element.9.refs_0_, bf16[256,2048]{1,0:T(8,128)(2,1)S(1)} %get-tuple-element.10.refs_1_, f32[256,128]{1,0:T(8,128)S(1)} %get-tuple-element.11.refs_2_), custom_call_target="tpu_custom_call" | custom-call | tf_op jit(solution)/shard_map/flush/pallas_call | solution.py:385

commit v6 on v5

--- a/solution.py
+++ b/solution.py
@@ -25,6 +25,7 @@
     return (x * 4 + half * 2 + core) * LANE
 
 
+PATIENT = 5
 AHEAD = 2
 SPANS = tuple((k, sum(CHUNKS[:k]), tiles) for k, tiles in enumerate(CHUNKS))
 
@@ -70,6 +71,7 @@
 ):
     rep, fsdp = lax.axis_index("rep"), lax.axis_index("fsdp")
     x, half, core = rep // 4, (rep // 2) % 2, rep % 2
+    late = jnp.logical_and(half == 1, fsdp % 8 >= PATIENT)
     own_column = pl.multiple_of(rep * LANE, LANE)
     other_column = pl.multiple_of((x * 4 + (1 - half) * 2 + core) * LANE, LANE)
 
@@ -231,10 +233,11 @@
             return carry
 
         lax.fori_loop(first, first + tiles, add, 0)
-
-        @pl.when(half == 1)
-        def _():
-            wait(z_in.at[span], z_recv.at[k])
+        if k == 0:
+
+            @pl.when(late)
+            def _():
+                wait(z_in.at[span], z_recv.at[k])
 
         start(z_out.at[span], z_in.at[span], z_send.at[k], z_recv.at[k], across)
 
@@ -268,9 +271,13 @@
 
     for k, first, tiles in SPANS:
         span = pl.ds(first, tiles)
-
-        @pl.when(half == 0)
-        def _():
+        if k == 0:
+
+            @pl.when(jnp.logical_not(late))
+            def _():
+                wait(z_in.at[span], z_recv.at[k])
+
+        else:
             wait(z_in.at[span], z_recv.at[k])
 
         def update(tile, carry):

time: 52.4 us -> 40.9 us (0.78)
  the two profiles are of different devices: /device:TPU:41 before, /device:TPU:1 now
where the time goes in v6:
time: 40.9 us; the launch traced here: 40.5 us
  Pallas kernels  39.8 us (97%)
  between operations  0.64 us (2%)
    pallas_call x1, Pallas kernels, on_device(): pl.pallas_call(exchange, out_shape=results, in_specs=[outside] * 4, out_s...  38.4 us
    pallas_call x1, Pallas kernels, on_device(): pl.pallas_call(flush, out_shape=results, in_specs=[anywhere] * 3, out_spe...  1.37 us

profile of v6, /device:TPU:1, one launch (start us, length us, event | category | flops | bytes accessed | tf_op | source)
XLA Modules:
  0.0 40.5 jit_solution(15977363823202645272)
XLA Ops:
  0.6 38.4 %exchange.1 = (bf16[256,2048]{1,0:T(8,128)(2,1)S(1)}, bf16[256,2048]{1,0:T(8,128)(2,1)S(1)}, f32[256,128]{1,0:T(8,128)S(1)}) custom-call(bf16[256,2048]{1,0:T(8,128)(2,1)} %bitcast.9, bf16[256,2048]{1,0:T(8,128)(2,1)} %bitcast.10, s32[64,256]{1,0:T(8,128)} %bitcast.12, f32[256,128]{1,0:T(8,128)} %bitcast.11), custom_call_target="tpu_custom_call" | custom-call | tf_op jit(solution)/shard_map/exchange/pallas_call | solution.py:347
  39.1 1.4 %flush.1 = (bf16[256,2048]{1,0:T(8,128)(2,1)}, bf16[256,2048]{1,0:T(8,128)(2,1)}, f32[256,128]{1,0:T(8,128)}) custom-call(bf16[256,2048]{1,0:T(8,128)(2,1)S(1)} %get-tuple-element.9.refs_0_, bf16[256,2048]{1,0:T(8,128)(2,1)S(1)} %get-tuple-element.10.refs_1_, f32[256,128]{1,0:T(8,128)S(1)} %get-tuple-element.11.refs_2_), custom_call_target="tpu_custom_call" | custom-call | tf_op jit(solution)/shard_map/flush/pallas_call | solution.py:392

commit v7 on v6

--- a/solution.py
+++ b/solution.py
@@ -26,6 +26,7 @@
 
 
 PATIENT = 5
+DIRECT = 1
 AHEAD = 2
 SPANS = tuple((k, sum(CHUNKS[:k]), tiles) for k, tiles in enumerate(CHUNKS))
 
@@ -196,10 +197,20 @@
                 pl.semaphore_wait(near_sem, 1)
 
         span = pl.ds(first, tiles)
-        start(
-            coded.at[1 - core, :, span], pair_in.at[:, span], core_send.at[k], core_recv.at[k], partner
-        )
-        if k >= AHEAD:
+        if k < DIRECT:
+            for slot in (1, 0, 2):
+                there, device = beside(slot + 1, 1 - core)
+                piece = coded.at[1 - core, there, span]
+                start(piece, pair_in.at[x, span], core_send.at[k], core_recv.at[k], device)
+                there, device = beside(slot + 1, core)
+                piece = coded.at[core, there, span]
+                start(piece, arrived.at[slot, span], rs_send.at[k], rs_recv.at[k], device)
+            piece = coded.at[1 - core, x, span]
+            start(piece, pair_in.at[x, span], core_send.at[k], core_recv.at[k], partner)
+        else:
+            pieces = coded.at[1 - core, :, span]
+            start(pieces, pair_in.at[:, span], core_send.at[k], core_recv.at[k], partner)
+        if k >= AHEAD + DIRECT:
             pass_pairs(k - AHEAD)
     for k in range(len(CHUNKS) - AHEAD, len(CHUNKS)):
         pass_pairs(k)
@@ -217,11 +228,20 @@
     for k, first, tiles in SPANS:
         span = pl.ds(first, tiles)
         wait(arrived.at[:, span], rs_recv.at[k])
+        if k < DIRECT:
+            wait(pair_in.at[:, span], core_recv.at[k])
 
         def add(tile, carry):
             rows = pl.ds(pl.multiple_of(tile * TILE, TILE), TILE)
-            own = pairs[x, tile, half].astype(jnp.float32)
-            other = pairs[x, tile, 1 - half].astype(jnp.float32)
+            if k < DIRECT:
+                own = coded[core, x, tile, half].astype(jnp.float32)
+                other = coded[core, x, tile, 1 - half].astype(jnp.float32)
+                for place in range(XS):
+                    own = own + pair_in[place, tile, half].astype(jnp.float32)
+                    other = other + pair_in[place, tile, 1 - half].astype(jnp.float32)
+            else:
+                own = pairs[x, tile, half].astype(jnp.float32)
+                other = pairs[x, tile, 1 - half].astype(jnp.float32)
             for slot in range(XS - 1):
                 own = own + arrived[slot, tile, half].astype(jnp.float32)
                 other = other + arrived[slot, tile, 1 - half].astype(jnp.float32)

time: 40.9 us -> 41.3 us (level)
  no operation moved by 1% of the time
where the time goes in v7:
time: 41.3 us; the launch traced here: 40.5 us
  Pallas kernels  39.8 us (96%)
  between operations  0.64 us (2%)
    pallas_call x1, Pallas kernels, on_device(): pl.pallas_call(exchange, out_shape=results, in_specs=[outside] * 4, out_s...  38.5 us
    pallas_call x1, Pallas kernels, on_device(): pl.pallas_call(flush, out_shape=results, in_specs=[anywhere] * 3, out_spe...  1.37 us

profile of v7, /device:TPU:1, one launch (start us, length us, event | category | flops | bytes accessed | tf_op | source)
XLA Modules:
  0.0 40.5 jit_solution(4761266443395498175)
XLA Ops:
  0.6 38.5 %exchange.1 = (bf16[256,2048]{1,0:T(8,128)(2,1)S(1)}, bf16[256,2048]{1,0:T(8,128)(2,1)S(1)}, f32[256,128]{1,0:T(8,128)S(1)}) custom-call(bf16[256,2048]{1,0:T(8,128)(2,1)} %bitcast.9, bf16[256,2048]{1,0:T(8,128)(2,1)} %bitcast.10, s32[64,256]{1,0:T(8,128)} %bitcast.12, f32[256,128]{1,0:T(8,128)} %bitcast.11), custom_call_target="tpu_custom_call" | custom-call | tf_op jit(solution)/shard_map/exchange/pallas_call | solution.py:367
  39.1 1.4 %flush.1 = (bf16[256,2048]{1,0:T(8,128)(2,1)}, bf16[256,2048]{1,0:T(8,128)(2,1)}, f32[256,128]{1,0:T(8,128)}) custom-call(bf16[256,2048]{1,0:T(8,128)(2,1)S(1)} %get-tuple-element.9.refs_0_, bf16[256,2048]{1,0:T(8,128)(2,1)S(1)} %get-tuple-element.10.refs_1_, f32[256,128]{1,0:T(8,128)S(1)} %get-tuple-element.11.refs_2_), custom_call_target="tpu_custom_call" | custom-call | tf_op jit(solution)/shard_map/flush/pallas_call | solution.py:412

commit v8 on v7

--- a/solution.py
+++ b/solution.py
@@ -15,7 +15,7 @@
 REPS = 16
 MINE, OTHER = 0.5, 0.7 * 1.9 / REPS
 BOUNDS = ((0.25, 0.5), (0.75, 1.0), (1.25, 1.5), (1.75, 2.0), (2.5, 3.0), (3.5, 4.0), (5.0, 6.0))
-CHUNKS = (1, 2, 3, 4, 3, 2, 1)
+CHUNKS = (1, 1, 2, 3, 3, 3, 2, 1)
 HOPS = len(CHUNKS) - 2
 PLACES = tuple((c, x, h) for c in range(2) for x in range(XS) for h in range(2))
 HEARD = 2 * XS - 1
@@ -25,7 +25,7 @@
     return (x * 4 + half * 2 + core) * LANE
 
 
-PATIENT = 5
+HELD = 4
 DIRECT = 1
 AHEAD = 2
 SPANS = tuple((k, sum(CHUNKS[:k]), tiles) for k, tiles in enumerate(CHUNKS))
@@ -72,7 +72,9 @@
 ):
     rep, fsdp = lax.axis_index("rep"), lax.axis_index("fsdp")
     x, half, core = rep // 4, (rep // 2) % 2, rep % 2
-    late = jnp.logical_and(half == 1, fsdp % 8 >= PATIENT)
+    pair = fsdp % 8
+    late = jnp.logical_and(half == 1, jnp.logical_or(pair == 5, pair == 7))
+    holds = jnp.logical_and(half == 1, pair == 6)
     own_column = pl.multiple_of(rep * LANE, LANE)
     other_column = pl.multiple_of((x * 4 + (1 - half) * 2 + core) * LANE, LANE)
 
@@ -223,6 +225,11 @@
     @pl.when(core == 0)
     def _():
         pl.semaphore_wait(far_sem, 1)
+
+    def cross(k):
+        _, first, tiles = SPANS[k]
+        span = pl.ds(first, tiles)
+        start(z_out.at[span], z_in.at[span], z_send.at[k], z_recv.at[k], across)
 
     small[1].wait()
     for k, first, tiles in SPANS:
@@ -259,7 +266,17 @@
             def _():
                 wait(z_in.at[span], z_recv.at[k])
 
-        start(z_out.at[span], z_in.at[span], z_send.at[k], z_recv.at[k], across)
+        if k == HELD:
+
+            @pl.when(holds)
+            def _():
+                for held in range(HELD):
+                    cross(held)
+
+        if k < HELD:
+            pl.when(jnp.logical_not(holds))(functools.partial(cross, k))
+        else:
+            cross(k)
 
     def hand_over(k):
         _, first, tiles = SPANS[k]

time: 41.3 us -> 40.7 us (0.985); the launches traced: 40.5 us -> 40.5 us
  no operation moved by 1% of the time
where the time goes in v8:
time: 40.7 us; the launch traced here: 40.5 us
  Pallas kernels  39.9 us (98%)
  between operations  0.64 us (2%)
    pallas_call x1, Pallas kernels, on_device(): pl.pallas_call(exchange, out_shape=results, in_specs=[outside] * 4, out_s...  38.5 us
    pallas_call x1, Pallas kernels, on_device(): pl.pallas_call(flush, out_shape=results, in_specs=[anywhere] * 3, out_spe...  1.37 us

profile of v8, /device:TPU:1, one launch (start us, length us, event | category | flops | bytes accessed | tf_op | source)
XLA Modules:
  0.0 40.5 jit_solution(10834700129206864045)
XLA Ops:
  0.6 38.5 %exchange.1 = (bf16[256,2048]{1,0:T(8,128)(2,1)S(1)}, bf16[256,2048]{1,0:T(8,128)(2,1)S(1)}, f32[256,128]{1,0:T(8,128)S(1)}) custom-call(bf16[256,2048]{1,0:T(8,128)(2,1)} %bitcast.9, bf16[256,2048]{1,0:T(8,128)(2,1)} %bitcast.10, s32[64,256]{1,0:T(8,128)} %bitcast.12, f32[256,128]{1,0:T(8,128)} %bitcast.11), custom_call_target="tpu_custom_call" | custom-call | tf_op jit(solution)/shard_map/exchange/pallas_call | solution.py:384
  39.2 1.4 %flush.1 = (bf16[256,2048]{1,0:T(8,128)(2,1)}, bf16[256,2048]{1,0:T(8,128)(2,1)}, f32[256,128]{1,0:T(8,128)}) custom-call(bf16[256,2048]{1,0:T(8,128)(2,1)S(1)} %get-tuple-element.9.refs_0_, bf16[256,2048]{1,0:T(8,128)(2,1)S(1)} %get-tuple-element.10.refs_1_, f32[256,128]{1,0:T(8,128)S(1)} %get-tuple-element.11.refs_2_), custom_call_target="tpu_custom_call" | custom-call | tf_op jit(solution)/shard_map/flush/pallas_call | solution.py:429

commit v9 on v8

--- a/solution.py
+++ b/solution.py
@@ -74,7 +74,8 @@
     x, half, core = rep // 4, (rep // 2) % 2, rep % 2
     pair = fsdp % 8
     late = jnp.logical_and(half == 1, jnp.logical_or(pair == 5, pair == 7))
-    holds = jnp.logical_and(half == 1, pair == 6)
+    held_pair = jnp.logical_or(pair == 6, jnp.logical_or(pair == 3, pair == 4))
+    holds = jnp.logical_and(half == 1, held_pair)
     own_column = pl.multiple_of(rep * LANE, LANE)
     other_column = pl.multiple_of((x * 4 + (1 - half) * 2 + core) * LANE, LANE)
 

time: 40.7 us -> 42.4 us (1.042)
  the two profiles are of different devices: /device:TPU:1 before, /device:TPU:57 now
where the time goes in v9:
time: 42.4 us; the launch traced here: 42.3 us
  Pallas kernels  41.6 us (98%)
  between operations  0.64 us (2%)
    pallas_call x1, Pallas kernels, on_device(): pl.pallas_call(exchange, out_shape=results, in_specs=[outside] * 4, out_s...  40.2 us
    pallas_call x1, Pallas kernels, on_device(): pl.pallas_call(flush, out_shape=results, in_specs=[anywhere] * 3, out_spe...  1.37 us

profile of v9, /device:TPU:57, one launch (start us, length us, event | category | flops | bytes accessed | tf_op | source)
XLA Modules:
  0.0 42.3 jit_solution(7100560770683160399)
XLA Ops:
  0.6 40.2 %exchange.1 = (bf16[256,2048]{1,0:T(8,128)(2,1)S(1)}, bf16[256,2048]{1,0:T(8,128)(2,1)S(1)}, f32[256,128]{1,0:T(8,128)S(1)}) custom-call(bf16[256,2048]{1,0:T(8,128)(2,1)} %bitcast.9, bf16[256,2048]{1,0:T(8,128)(2,1)} %bitcast.10, s32[64,256]{1,0:T(8,128)} %bitcast.12, f32[256,128]{1,0:T(8,128)} %bitcast.11), custom_call_target="tpu_custom_call" | custom-call | tf_op jit(solution)/shard_map/exchange/pallas_call | solution.py:385
  40.9 1.4 %flush.1 = (bf16[256,2048]{1,0:T(8,128)(2,1)}, bf16[256,2048]{1,0:T(8,128)(2,1)}, f32[256,128]{1,0:T(8,128)}) custom-call(bf16[256,2048]{1,0:T(8,128)(2,1)S(1)} %get-tuple-element.9.refs_0_, bf16[256,2048]{1,0:T(8,128)(2,1)S(1)} %get-tuple-element.10.refs_1_, f32[256,128]{1,0:T(8,128)S(1)} %get-tuple-element.11.refs_2_), custom_call_target="tpu_custom_call" | custom-call | tf_op jit(solution)/shard_map/flush/pallas_call | solution.py:430
